TPU v7x, 32 devices: a whole 2x2x4 slice. The times are simulated.
32 devices in a mesh: tm: 8 (over y, x, core), cell: 4 (over z).
Axes of the slice: x: 2, y: 2, z: 4, core: 2. Of those that a mesh axis runs over, the one named last changes fastest.
Arguments:
- theta: float32 [3, 1024, 32], P(None, 'cell', 'tm'), may hold values from -0.6 to 0.6
- tangent: float32 [3, 1024, 32], P(None, 'cell', 'tm'), may hold values from -6 to 6
- covariates: float32 [3, 2048, 4096], P(None, 'cell', 'tm'), may hold values from -4 to 4
- counts: int32 [2048, 4096], P('cell', 'tm'), may hold values from 0 to 5
- sfirst: int32 [2048], P('cell'), may hold values from 0 to 1008, as said below
- sweight: float32 [16, 2048], P(None, 'cell'), may hold values from 0.05 to 1
- tfirst: int32 [4096], P('tm'), may hold values from 0 to 28, as said below
- tweight: float32 [4, 4096], P(None, 'tm'), may hold values from 0.05 to 1
Outputs:
- hess_vec: float32 [3, 1024, 32], P(None, 'cell', 'tm')
- gradient: float32 [3, 1024, 32], P(None, 'cell', 'tm')
Inputs may be any that keep to these rules, and one draw needn't show every extreme that they name: Cell c's support block sfirst[c] to sfirst[c] + 15 lies within the basis functions (c // 512) * 256 - 16 to (c // 512 + 1) * 256 + 15. Hour h's support block tfirst[h] to tfirst[h] + 3 lies within the basis functions (h // 512) * 4 - 2 to (h // 512 + 1) * 4 + 1.
All inputs are finite; a program needn't handle non-finite values.
Results may differ from a plain program's by a relative error of at most 0.0002.
Values sent between devices are 32-bit elements; how exact they have to be, the bound alone decides.
A program may use at most 64 MiB of HBM per device.

v0:
```python
import jax
import jax.numpy as jnp
from jax import lax
from jax.sharding import PartitionSpec as P

WS = 16
HS = 16
HT = 2


def with_halo(cells, sides, width):
    for axis, dim in sides:
        count = lax.axis_size(axis)
        ends = count - 1
        head = lax.slice_in_dim(cells, 0, width, axis=dim)
        tail = lax.slice_in_dim(cells, cells.shape[dim] - width, cells.shape[dim], axis=dim)
        cells = jnp.concatenate(
            [
                lax.ppermute(tail, axis, [(i, (i + 1) % count) for i in range(ends)]),
                cells,
                lax.ppermute(head, axis, [((i + 1) % count, i) for i in range(ends)]),
            ],
            axis=dim,
        )
    return cells


def from_behind(value, axis, steps):
    count = lax.axis_size(axis)
    first, last = (max(0, -steps), min(count, count - steps))
    return lax.ppermute(value, axis, [(source, source + steps) for source in range(first, last)])


def basis_block(first, values, row_total, offset):
    diffs = jnp.arange(row_total, dtype=jnp.int32)[:, None] - (first - offset)[None, :]
    result = jnp.zeros((row_total, first.shape[0]), jnp.float32)
    for index in range(values.shape[0]):
        result = result + jnp.where(diffs == index, values[index][None, :], jnp.float32(0.0))
    return result


def body(theta, tangent, covariates, counts, sfirst, sweight, tfirst, tweight):
    high = lax.Precision.HIGHEST
    row_count = theta.shape[1]
    col_count = theta.shape[2]
    hour_count = covariates.shape[2]
    stacked = jnp.stack([theta, tangent])
    widened = with_halo(stacked, (("tm", 3),), HT)
    col_start = lax.axis_index("tm") * col_count - HT
    extended = with_halo(widened, (("cell", 2),), HS)
    row_start = lax.axis_index("cell") * row_count - HS
    space_basis = basis_block(sfirst, sweight, row_count + 2 * HS, row_start)
    time_basis = basis_block(tfirst, tweight, widened.shape[3], col_start)
    spatial = jnp.einsum("sc,pkst->pkct", space_basis, extended, precision=high)
    fields = jnp.einsum("pkct,th->pkch", spatial, time_basis, precision=high)
    predictor = jnp.sum(covariates * fields[0], axis=0)
    tangent_pred = jnp.sum(covariates * fields[1], axis=0)
    rates = jnp.exp(predictor)
    weighted = jnp.stack(
        [
            covariates * (rates * tangent_pred)[None],
            covariates * (counts.astype(jnp.float32) - rates)[None],
        ]
    )
    time_part = jnp.einsum("pkch,th->pkct", weighted, time_basis, precision=high)
    col_pad = ((0, 0), (0, 0), (0, 0), (0, col_count - HT))
    col_pad_high = ((0, 0), (0, 0), (0, 0), (col_count - HT, 0))
    middle = time_part[..., HT : HT + col_count]
    lower = from_behind(time_part[..., col_count + HT :], "tm", 1)
    upper = from_behind(time_part[..., :HT], "tm", -1)
    time_part = middle + jnp.pad(lower, col_pad) + jnp.pad(upper, col_pad_high)
    partial_value = jnp.einsum("sc,pkct->pkst", space_basis, time_part, precision=high)
    own_rows = partial_value[:, :, HS : HS + row_count]
    from_below = from_behind(partial_value[:, :, row_count + HS :], "cell", 1)
    from_above = from_behind(partial_value[:, :, :HS], "cell", -1)
    own_rows = own_rows + jnp.pad(from_below, ((0, 0), (0, 0), (0, row_count - HS), (0, 0)))
    own_rows = own_rows + jnp.pad(from_above, ((0, 0), (0, 0), (row_count - HS, 0), (0, 0)))
    hess_vec = own_rows[0] / jnp.float32(WS * (hour_count // col_count))
    gradient = own_rows[1] / jnp.float32(hour_count // col_count)
    return (hess_vec, gradient)


def solution(mesh):
    return jax.shard_map(
        body,
        mesh=mesh,
        in_specs=(
            P(None, "cell", "tm"),
            P(None, "cell", "tm"),
            P(None, "cell", "tm"),
            P("cell", "tm"),
            P("cell"),
            P(None, "cell"),
            P("tm"),
            P(None, "tm"),
        ),
        out_specs=(P(None, "cell", "tm"), P(None, "cell", "tm")),
        check_vma=False,
    )
```

profile of v0, /device:TPU:11, one launch (start us, length us, event | category | flops | bytes accessed | tf_op | source)
XLA Modules:
  0.0 55.6 jit_solution(15083117918785293718)
XLA Ops:
  0.6 0.8 %fusion.49 = (f32[2,3,256,2]{2,3,1,0:T(2,128)S(1)}, f32[2,3,256,2]{2,3,1,0:T(2,128)S(1)}) fusion(f32[1,3,256,4]{2,3,1,0:T(4,128)} %bitcast.61, f32[1,3,256,4]{2,3,1,0:T(4,128)} %bitcast.64), kind=kLoop, calls=%fused_computation.65 | loop fusion | flops 6144 | bytes 49152 | tf_op jit(solution)/shard_map/stack | solution.py:47
  1.4 3.7 %collective-permute-start = (f32[2,3,256,2]{2,3,1,0:T(2,128)S(1)}, f32[2,3,256,2]{2,3,1,0:T(2,128)S(1)}, u32[]{:S(2)}, u32[]{:S(2)}) collective-permute-start(f32[2,3,256,2]{2,3,1,0:T(2,128)S(1)} %get-tuple-element.32), channel_id=1, source_target_pairs={{0,4},{4,8},{8,12},{12,16},{16,20},{20,24},{24,28},{1,5},{5,9},{9,... | collective-permute-start | bytes 36872 | tf_op jit(solution)/shard_map/ppermute | solution.py:19
  5.1 1.9 %collective-permute-start.1 = (f32[2,3,256,2]{2,3,1,0:T(2,128)S(1)}, f32[2,3,256,2]{2,3,1,0:T(2,128)S(1)}, u32[]{:S(2)}, u32[]{:S(2)}) collective-permute-start(f32[2,3,256,2]{2,3,1,0:T(2,128)S(1)} %get-tuple-element.33), channel_id=1, source_target_pairs={{4,0},{8,4},{12,8},{16,12},{20,16},{24,20},{28,24},{5,1},{9,5},{13... | collective-permute-start | bytes 36872 | tf_op jit(solution)/shard_map/ppermute | solution.py:21
  7.1 0.9 %fusion.122 = (f32[1,512]{1,0:T(1,128)S(1)}, f32[1,512]{1,0:T(1,128)S(1)}, f32[1,512]{1,0:T(1,128)S(1)}, f32[1,512]{1,0:T(1,128)S(1)}) fusion(f32[4,512]{1,0:T(4,128)} %param.15), kind=kLoop, calls=%fused_computation.143 | loop fusion | bytes 16384 | tf_op jit(solution)/shard_map/slice | solution.py:38
  7.9 1.1 %fusion.121 = (f32[1,512]{1,0:T(1,128)S(1)}, f32[1,512]{1,0:T(1,128)S(1)}, f32[1,512]{1,0:T(1,128)S(1)}, f32[1,512]{1,0:T(1,128)S(1)}, f32[1,512]{1,0:T(1,128)S(...) fusion(f32[16,512]{1,0:T(8,128)} %param.13), kind=kLoop, calls=%fused_computation.142 | loop fusion | bytes 65536 | tf_op jit(solution)/shard_map/slice | solution.py:38
  9.0 0.7 %broadcast_subtract_fusion.1 = s32[512]{0:T(512)S(1)} fusion(s32[512]{0:T(512)} %param.12, s32[]{:T(128)S(6)} %sub.48), kind=kLoop, calls=%fused_computation.92 | loop fusion | flops 512 | bytes 4100 | tf_op jit(solution)/shard_map/sub | solution.py:35
  9.7 1.3 %collective-permute-done.1 = f32[2,3,256,2]{2,3,1,0:T(2,128)S(1)} collective-permute-done((f32[2,3,256,2]{2,3,1,0:T(2,128)S(1)}, f32[2,3,256,2]{2,3,1,0:T(2,128)S(1)}, u32[]{:S(2)}, u32[]{:S(2)}) %collective-permute-start.1) | collective-permute-done | bytes 12320 | tf_op jit(solution)/shard_map/ppermute | solution.py:21
  11.0 0.7 %pad_maximum_fusion = f32[2,3,256,8]{2,3,1,0:T(8,128)S(1)} fusion(f32[2,3,256,2]{2,3,1,0:T(2,128)S(1)} %collective-permute-done.1, f32[1,3,256,4]{2,3,1,0:T(4,128)} %bitcast.65, f32[1,3,256,4]{2,3,1,0:T(4,128)} %bitcast.62, f32[2,3,256,2]{2,3,1,0:T(2,128)S(1)} %collective-permute-done), kind=kLoop, calls=%fused_computation.49 | loop fusion | flops 36864 | bytes 98304 | tf_op jit(solution)/shard_map/concatenate | solution.py:17
  11.8 0.1 fusion.119
  11.9 3.2 %collective-permute-start.2 = (f32[2,3,16,8]{2,3,1,0:T(8,128)S(1)}, f32[2,3,16,8]{2,3,1,0:T(8,128)S(1)}, u32[]{:S(2)}, u32[]{:S(2)}) collective-permute-start(f32[2,3,16,8]{2,3,1,0:T(8,128)S(1)} %get-tuple-element.10), channel_id=1, source_target_pairs={{0,1},{1,2},{2,3},{4,5},{5,6},{6,7},{8,9},{9,10},{10,11},{12,13},{... | collective-permute-start | bytes 9224 | tf_op jit(solution)/shard_map/ppermute | solution.py:19
  15.1 2.1 %collective-permute-start.3 = (f32[2,3,16,8]{2,3,1,0:T(8,128)S(1)}, f32[2,3,16,8]{2,3,1,0:T(8,128)S(1)}, u32[]{:S(2)}, u32[]{:S(2)}) collective-permute-start(f32[2,3,16,8]{2,3,1,0:T(8,128)S(1)} %get-tuple-element.11), channel_id=1, source_target_pairs={{1,0},{2,1},{3,2},{5,4},{6,5},{7,6},{9,8},{10,9},{11,10},{13,12},{... | collective-permute-start | bytes 9224 | tf_op jit(solution)/shard_map/ppermute | solution.py:21
  17.1 0.7 %broadcast_subtract_fusion = s32[512]{0:T(512)S(1)} fusion(s32[512]{0:T(512)} %param.14, s32[]{:T(128)S(6)} %sub.54), kind=kLoop, calls=%fused_computation.91 | loop fusion | flops 512 | bytes 4100 | tf_op jit(solution)/shard_map/sub | solution.py:35
  17.8 2.3 %collective-permute-done.3 = f32[2,3,16,8]{2,3,1,0:T(8,128)S(1)} collective-permute-done((f32[2,3,16,8]{2,3,1,0:T(8,128)S(1)}, f32[2,3,16,8]{2,3,1,0:T(8,128)S(1)}, u32[]{:S(2)}, u32[]{:S(2)}) %collective-permute-start.3) | collective-permute-done | bytes 3104 | tf_op jit(solution)/shard_map/ppermute | solution.py:21
  20.1 2.2 %convolution_bitcast_fusion = f32[2,3,512,8]{2,3,1,0:T(8,128)S(1)} fusion(f32[512]{0:T(512)S(1)} %bitcast.103, f32[512]{0:T(512)S(1)} %bitcast.105, f32[512]{0:T(512)S(1)} %bitcast.77, f32[512]{0:T(512)S(1)} %bitcast.79, f32[512]{0:T(512)S(1)} %bitcast.81, f32[512]{0:T(512)S(1)} %bitcast.83, f32[512]{0:T(512)S(1)} %bitcast.85, f32[512]{0:T(512)S(1)} %bitcast.87, ...), kind=kOutput, calls=%fused_computation.12 | convolution fusion | flops 92081664 | bytes 188416 | tf_op jit(solution)/shard_map/sc,pkst->pkct/dot_general | solution.py:54
  22.4 0.0 copy-start
  22.4 5.1 %fusion.43 = f32[2,3,512,512]{3,2,1,0:T(8,128)S(1)} fusion(f32[2,3,512,8]{2,3,1,0:T(8,128)S(1)} %convolution_bitcast_fusion, f32[512]{0:T(512)S(1)} %bitcast.71, f32[512]{0:T(512)S(1)} %bitcast.73, f32[512]{0:T(512)S(1)} %bitcast.69, f32[512]{0:T(512)S(1)} %bitcast.67, s32[512]{0:T(512)S(1)} %broadcast_subtract_fusion), kind=kOutput, calls=%fused_computation.57 | convolution fusion | flops 151044096 | bytes 6400000 | tf_op jit(solution)/shard_map/pkct,th->pkch/dot_general | solution.py:55
  27.5 0.0 copy-start.1
  27.5 1.3 %fusion.5 = (f32[512,512]{1,0:T(8,128)S(1)}, f32[512,512]{1,0:T(8,128)S(1)}) fusion(f32[3,512,512]{2,1,0:T(8,128)S(1)} %copy-done, f32[2,3,512,512]{3,2,1,0:T(8,128)S(1)} %fusion.43), kind=kLoop, calls=%fused_computation.6 | loop fusion | flops 2621440 | bytes 11534336 | tf_op jit(solution)/shard_map/reduce_sum | solution.py:57
  28.8 0.4 exponential_multiply_fusion
  29.2 0.9 %multiply_bitcast_fusion.1 = (f32[1,3,512,512]{3,2,1,0:T(8,128)S(1)}, f32[1,3,512,512]{3,2,1,0:T(8,128)S(1)}) fusion(f32[3,512,512]{2,1,0:T(8,128)S(1)} %copy-done, f32[512,512]{1,0:T(8,128)S(1)} %get-tuple-element.6, f32[512,512]{1,0:T(8,128)S(1)} %get-tuple-element.7), kind=kLoop, calls=%fused_computation.11 | loop fusion | flops 1572864 | bytes 11534336 | tf_op jit(solution)/shard_map/stack | solution.py:59
  30.1 5.3 %fusion = f32[2,3,512,8]{2,3,1,0:T(8,128)S(1)} fusion(f32[1,3,512,512]{3,2,1,0:T(8,128)S(1)} %get-tuple-element.5, f32[1,3,512,512]{3,2,1,0:T(8,128)S(1)} %get-tuple-element.4, f32[512]{0:T(512)S(1)} %bitcast.72, f32[512]{0:T(512)S(1)} %bitcast.74, f32[512]{0:T(512)S(1)} %bitcast.70, f32[512]{0:T(512)S(1)} %bitcast.68, s32[512]{0:T(512)S(1)} %broadcast_subtract_fusion), kind=kOutput, calls=%fused_computation | convolution fusion | flops 152616960 | bytes 6400000 | tf_op jit(solution)/shard_map/pkch,th->pkct/dot_general | solution.py:65
  35.4 4.1 %collective-permute-start.4 = (f32[2,3,512,2]{2,3,1,0:T(2,128)S(1)}, f32[2,3,512,2]{2,3,1,0:T(2,128)S(1)}, u32[]{:S(2)}, u32[]{:S(2)}) collective-permute-start(f32[2,3,512,2]{2,3,1,0:T(2,128)S(1)} %get-tuple-element.8), channel_id=1, source_target_pairs={{0,4},{4,8},{8,12},{12,16},{16,20},{20,24},{24,28},{1,5},{5,9},{9,... | collective-permute-start | bytes 73736 | tf_op jit(solution)/shard_map/ppermute | solution.py:31
  39.6 1.9 %collective-permute-start.5 = (f32[2,3,512,2]{2,3,1,0:T(2,128)S(1)}, f32[2,3,512,2]{2,3,1,0:T(2,128)S(1)}, u32[]{:S(2)}, u32[]{:S(2)}) collective-permute-start(f32[2,3,512,2]{2,3,1,0:T(2,128)S(1)} %get-tuple-element.9), channel_id=1, source_target_pairs={{4,0},{8,4},{12,8},{16,12},{20,16},{24,20},{28,24},{5,1},{9,5},{13... | collective-permute-start | bytes 73736 | tf_op jit(solution)/shard_map/ppermute | solution.py:31
  41.5 0.0 collective-permute-done.4
  41.5 4.1 %collective-permute-done.5 = f32[2,3,512,2]{2,3,1,0:T(2,128)S(1)} collective-permute-done((f32[2,3,512,2]{2,3,1,0:T(2,128)S(1)}, f32[2,3,512,2]{2,3,1,0:T(2,128)S(1)}, u32[]{:S(2)}, u32[]{:S(2)}) %collective-permute-start.5) | collective-permute-done | bytes 24608 | tf_op jit(solution)/shard_map/ppermute | solution.py:31
  45.6 1.6 %convolution_bitcast_fusion.1 = f32[2,3,288,4]{2,3,1,0:T(4,128)S(1)} fusion(f32[512]{0:T(512)S(1)} %bitcast.104, f32[512]{0:T(512)S(1)} %bitcast.106, f32[512]{0:T(512)S(1)} %bitcast.78, f32[512]{0:T(512)S(1)} %bitcast.80, f32[512]{0:T(512)S(1)} %bitcast.82, f32[512]{0:T(512)S(1)} %bitcast.84, f32[512]{0:T(512)S(1)} %bitcast.86, f32[512]{0:T(512)S(1)} %bitcast.88, ...), kind=kOutput, calls=%fused_computation.13 | convolution fusion | flops 49569792 | bytes 160768 | tf_op jit(solution)/shard_map/sc,pkct->pkst/dot_general | solution.py:72
  47.2 0.1 fusion.120
  47.3 3.2 %collective-permute-start.6 = (f32[2,3,16,4]{2,3,1,0:T(4,128)S(1)}, f32[2,3,16,4]{2,3,1,0:T(4,128)S(1)}, u32[]{:S(2)}, u32[]{:S(2)}) collective-permute-start(f32[2,3,16,4]{2,3,1,0:T(4,128)S(1)} %get-tuple-element.12), channel_id=1, source_target_pairs={{0,1},{1,2},{2,3},{4,5},{5,6},{6,7},{8,9},{9,10},{10,11},{12,13},{... | collective-permute-start | bytes 4616 | tf_op jit(solution)/shard_map/ppermute | solution.py:31
  50.5 2.1 %collective-permute-start.7 = (f32[2,3,16,4]{2,3,1,0:T(4,128)S(1)}, f32[2,3,16,4]{2,3,1,0:T(4,128)S(1)}, u32[]{:S(2)}, u32[]{:S(2)}) collective-permute-start(f32[2,3,16,4]{2,3,1,0:T(4,128)S(1)} %get-tuple-element.13), channel_id=1, source_target_pairs={{1,0},{2,1},{3,2},{5,4},{6,5},{7,6},{9,8},{10,9},{11,10},{13,12},{... | collective-permute-start | bytes 4616 | tf_op jit(solution)/shard_map/ppermute | solution.py:31
  52.6 2.3 %collective-permute-done.7 = f32[2,3,16,4]{2,3,1,0:T(4,128)S(1)} collective-permute-done((f32[2,3,16,4]{2,3,1,0:T(4,128)S(1)}, f32[2,3,16,4]{2,3,1,0:T(4,128)S(1)}, u32[]{:S(2)}, u32[]{:S(2)}) %collective-permute-start.7) | collective-permute-done | bytes 1568 | tf_op jit(solution)/shard_map/ppermute | solution.py:31
  54.9 0.1 fusion.41
  55.0 0.6 %fusion.50 = (f32[3,256,4]{1,2,0:T(4,128)}, f32[3,256,4]{1,2,0:T(4,128)}) fusion(f32[2,3,256,4]{2,3,1,0:T(4,128)S(1)} %fusion.41), kind=kLoop, calls=%fused_computation.67 | loop fusion | flops 6144 | bytes 49152 | tf_op jit(solution)/shard_map/div | solution.py:79
  (6 shorter events, 0.0 us)
Async XLA Ops:
  1.4 8.3 %collective-permute-start = (f32[2,3,256,2]{2,3,1,0:T(2,128)S(1)}, f32[2,3,256,2]{2,3,1,0:T(2,128)S(1)}, u32[]{:S(2)}, u32[]{:S(2)}) collective-permute-start(f32[2,3,256,2]{2,3,1,0:T(2,128)S(1)} %get-tuple-element.32), channel_id=1, source_target_pairs={{0,4},{4,8},{8,12},{12,16},{16,20},{20,24},{24,28},{1,5},{5,9},{9,... | collective-permute-start | bytes 36872 | tf_op jit(solution)/shard_map/ppermute | solution.py:19
  5.1 5.9 %collective-permute-start.1 = (f32[2,3,256,2]{2,3,1,0:T(2,128)S(1)}, f32[2,3,256,2]{2,3,1,0:T(2,128)S(1)}, u32[]{:S(2)}, u32[]{:S(2)}) collective-permute-start(f32[2,3,256,2]{2,3,1,0:T(2,128)S(1)} %get-tuple-element.33), channel_id=1, source_target_pairs={{4,0},{8,4},{12,8},{16,12},{20,16},{24,20},{28,24},{5,1},{9,5},{13... | collective-permute-start | bytes 36872 | tf_op jit(solution)/shard_map/ppermute | solution.py:21
  11.9 6.0 %collective-permute-start.2 = (f32[2,3,16,8]{2,3,1,0:T(8,128)S(1)}, f32[2,3,16,8]{2,3,1,0:T(8,128)S(1)}, u32[]{:S(2)}, u32[]{:S(2)}) collective-permute-start(f32[2,3,16,8]{2,3,1,0:T(8,128)S(1)} %get-tuple-element.10), channel_id=1, source_target_pairs={{0,1},{1,2},{2,3},{4,5},{5,6},{6,7},{8,9},{9,10},{10,11},{12,13},{... | collective-permute-start | bytes 9224 | tf_op jit(solution)/shard_map/ppermute | solution.py:19
  15.1 5.1 %collective-permute-start.3 = (f32[2,3,16,8]{2,3,1,0:T(8,128)S(1)}, f32[2,3,16,8]{2,3,1,0:T(8,128)S(1)}, u32[]{:S(2)}, u32[]{:S(2)}) collective-permute-start(f32[2,3,16,8]{2,3,1,0:T(8,128)S(1)} %get-tuple-element.11), channel_id=1, source_target_pairs={{1,0},{2,1},{3,2},{5,4},{6,5},{7,6},{9,8},{10,9},{11,10},{13,12},{... | collective-permute-start | bytes 9224 | tf_op jit(solution)/shard_map/ppermute | solution.py:21
  22.4 5.1 %copy-start = (f32[3,512,512]{2,1,0:T(8,128)S(1)}, f32[3,512,512]{2,1,0:T(8,128)}, u32[]{:S(2)}) copy-start(f32[3,512,512]{2,1,0:T(8,128)} %param.10) | copy-start | bytes 9437188
  27.5 1.3 %copy-start.1 = (s32[512,512]{1,0:T(8,128)S(1)}, s32[512,512]{1,0:T(8,128)}, u32[]{:S(2)}) copy-start(s32[512,512]{1,0:T(8,128)} %param.11) | copy-start | bytes 3145732
  35.4 6.1 %collective-permute-start.4 = (f32[2,3,512,2]{2,3,1,0:T(2,128)S(1)}, f32[2,3,512,2]{2,3,1,0:T(2,128)S(1)}, u32[]{:S(2)}, u32[]{:S(2)}) collective-permute-start(f32[2,3,512,2]{2,3,1,0:T(2,128)S(1)} %get-tuple-element.8), channel_id=1, source_target_pairs={{0,4},{4,8},{8,12},{12,16},{16,20},{20,24},{24,28},{1,5},{5,9},{9,... | collective-permute-start | bytes 73736 | tf_op jit(solution)/shard_map/ppermute | solution.py:31
  39.6 6.0 %collective-permute-start.5 = (f32[2,3,512,2]{2,3,1,0:T(2,128)S(1)}, f32[2,3,512,2]{2,3,1,0:T(2,128)S(1)}, u32[]{:S(2)}, u32[]{:S(2)}) collective-permute-start(f32[2,3,512,2]{2,3,1,0:T(2,128)S(1)} %get-tuple-element.9), channel_id=1, source_target_pairs={{4,0},{8,4},{12,8},{16,12},{20,16},{24,20},{28,24},{5,1},{9,5},{13... | collective-permute-start | bytes 73736 | tf_op jit(solution)/shard_map/ppermute | solution.py:31
  47.3 5.3 %collective-permute-start.6 = (f32[2,3,16,4]{2,3,1,0:T(4,128)S(1)}, f32[2,3,16,4]{2,3,1,0:T(4,128)S(1)}, u32[]{:S(2)}, u32[]{:S(2)}) collective-permute-start(f32[2,3,16,4]{2,3,1,0:T(4,128)S(1)} %get-tuple-element.12), channel_id=1, source_target_pairs={{0,1},{1,2},{2,3},{4,5},{5,6},{6,7},{8,9},{9,10},{10,11},{12,13},{... | collective-permute-start | bytes 4616 | tf_op jit(solution)/shard_map/ppermute | solution.py:31
  50.5 4.4 %collective-permute-start.7 = (f32[2,3,16,4]{2,3,1,0:T(4,128)S(1)}, f32[2,3,16,4]{2,3,1,0:T(4,128)S(1)}, u32[]{:S(2)}, u32[]{:S(2)}) collective-permute-start(f32[2,3,16,4]{2,3,1,0:T(4,128)S(1)} %get-tuple-element.13), channel_id=1, source_target_pairs={{1,0},{2,1},{3,2},{5,4},{6,5},{7,6},{9,8},{10,9},{11,10},{13,12},{... | collective-permute-start | bytes 4616 | tf_op jit(solution)/shard_map/ppermute | solution.py:31
where the time goes:
time: 56.6 us; the launch traced here: 55.6 us
  starting transfers between devices  22.2 us (39%)
  matrix products  14.2 us (25%)
  waiting for transfers between devices  10.1 us (18%)
  other arithmetic  6.17 us (11%)
  local copies, waits for them, and re-layouts  2.13 us (4%)
  between operations  0.83 us (1%)
    ppermute x4, starting transfers between devices, from_behind(): lax.ppermute(value, axis, [(source, source + steps) for source in range(f...  11.3 us
    ppermute x2, starting transfers between devices, with_halo(): lax.ppermute(tail, axis, [(i, (i + 1) % count) for i in range(ends)])  6.88 us
    ppermute x4, waiting for transfers between devices, from_behind(): lax.ppermute(value, axis, [(source, source + steps) for source in range(f...  6.46 us
    dot_general x1, matrix products, body(): jnp.einsum('pkch,th->pkct', weighted, time_basis, precision=high)  5.3 us
    dot_general x1, matrix products, body(): fields = jnp.einsum('pkct,th->pkch', spatial, time_basis, precision=high)  5.09 us
    ppermute x2, starting transfers between devices, with_halo(): lax.ppermute(head, axis, [((i + 1) % count, i) for i in range(ends)])  4 us
    ppermute x2, waiting for transfers between devices, with_halo(): lax.ppermute(head, axis, [((i + 1) % count, i) for i in range(ends)])  3.64 us
    dot_general x1, matrix products, body(): spatial = jnp.einsum('sc,pkst->pkct', space_basis, extended, precision=high)  2.2 us
  transfers between devices with their start and end apart: 8, of which 4 were waited for; matrix products, arithmetic and copies ran while one was open for 6% of the time, Pallas kernels for 0%

commit v1 on v0

v1 whole, which is shorter than its diff:
```python
import functools

import jax
import jax.numpy as jnp
from jax import lax
from jax.experimental import pallas as pl
from jax.experimental.pallas import tpu as pltpu
from jax.sharding import PartitionSpec as P

HS = 16
HT = 2
LANES = 128
SUB = 8
CHUNK = 128
MESH = pl.DeviceIdType.MESH
DIRS = [(dt, dc) for dt in (1, -1, 0) for dc in (0, 1, -1) if (dt, dc) != (0, 0)]
F32 = jnp.float32
BF16 = jnp.bfloat16


def split(value):
    head = value.astype(BF16).astype(F32)
    return head, value - head


def bf16_dot(left, right):
    return lax.dot_general(left, right, (((1,), (0,)), ((), ())), preferred_element_type=F32)


def kernel(
    nt, nc, theta_h, tangent_h, covar_h, counts_h, sfirst_h, sweight_h, tfirst_h, tweight_h, out_ref,
    theta, tangent, covar, counts, sfirst, sweight, tfirst, tweight,
    own, low, high, space_head, space_rest, time_rows, time_cols, back,
    res_own, res_edge, got, load_sem, chunk_sem, send_sem, recv_sem, back_send, back_recv,
):
    covs, td, sd = theta.shape
    cd, hd = counts.shape
    te = td + 2 * HT
    rows = te * SUB
    chunks = cd // CHUNK
    me_t, me_c = lax.axis_index("tm"), lax.axis_index("cell")

    loads = []
    for i, (src, dst) in enumerate(
        [(theta_h, theta), (tangent_h, tangent), (tfirst_h, tfirst), (tweight_h, tweight), (sfirst_h, sfirst), (sweight_h, sweight)]
    ):
        loads.append(pltpu.make_async_copy(src, dst, load_sem.at[i]))
        loads[-1].start()
    chunk_loads = []
    for i in range(chunks):
        part = pl.ds(i * CHUNK, CHUNK)
        pair = (
            pltpu.make_async_copy(covar_h.at[:, part], covar.at[:, part], chunk_sem.at[0, i]),
            pltpu.make_async_copy(counts_h.at[part], counts.at[part], chunk_sem.at[1, i]),
        )
        for copy in pair:
            copy.start()
        chunk_loads.append(pair)

    def there(dt, dc):
        inside = me_t >= 0
        if dt:
            inside = jnp.logical_and(inside, (me_t < nt - 1) if dt > 0 else (me_t > 0))
        if dc:
            inside = jnp.logical_and(inside, (me_c < nc - 1) if dc > 0 else (me_c > 0))
        return inside

    def device(dt, dc):
        return {"tm": me_t + dt, "cell": me_c + dc}

    for ref in [own, low, high] + got:
        ref[...] = jnp.zeros(ref.shape, F32)
    barrier = pltpu.get_barrier_semaphore()
    for dt, dc in DIRS:
        @pl.when(there(dt, dc))
        def _(dt=dt, dc=dc):
            pl.semaphore_signal(barrier, inc=1, device_id=device(dt, dc), device_id_type=MESH)

    loads[0].wait()
    loads[1].wait()
    for p, ref in enumerate((theta, tangent)):
        for k in range(covs):
            own[0:td, p * covs + k, :] = ref[k]

    loads[2].wait()
    loads[3].wait()
    index = lax.broadcasted_iota(jnp.int32, (rows, hd), 0) // SUB
    place = jnp.where(index < td, index, jnp.where(index < td + HT, index - (td + HT), index - HT)) + me_t * td
    diffs = place - tfirst[...]
    basis = jnp.zeros((rows, hd), F32)
    for j in range(tweight.shape[0]):
        basis = jnp.where(diffs == j, tweight[j : j + 1, :], basis)
    head, rest = split(basis)
    both = jnp.concatenate([head, rest], axis=0)
    time_cols[...] = both.T.astype(BF16)
    head, rest = head.astype(BF16), rest.astype(BF16)
    time_rows[...] = jnp.concatenate([head, head, rest, rest], axis=0)

    beside_t = (me_t > 0).astype(jnp.int32) + (me_t < nt - 1).astype(jnp.int32)
    beside_c = (me_c > 0).astype(jnp.int32) + (me_c < nc - 1).astype(jnp.int32)
    pl.semaphore_wait(barrier, (beside_t + 1) * (beside_c + 1) - 1)

    def forward(i, dt, dc):
        src_t = {0: pl.ds(0, td), 1: pl.ds(td - HT, HT), -1: pl.ds(0, HT)}[dt]
        dst_t = {0: pl.ds(0, td), 1: pl.ds(td, HT), -1: pl.ds(td + HT, HT)}[dt]
        src_s = {0: pl.ds(0, sd), 1: pl.ds(sd - LANES, LANES), -1: pl.ds(0, LANES)}[dc]
        dst = {0: own, 1: low, -1: high}[dc]
        return pltpu.make_async_remote_copy(
            src_ref=own.at[src_t, :, src_s], dst_ref=dst.at[dst_t],
            send_sem=send_sem.at[i], recv_sem=recv_sem.at[i], device_id=device(dt, dc), device_id_type=MESH,
        )

    for i, (dt, dc) in enumerate(DIRS):
        @pl.when(there(dt, dc))
        def _(i=i, dt=dt, dc=dc):
            forward(i, dt, dc).start()

    loads[4].wait()
    loads[5].wait()
    first = sfirst[...]
    support = sweight.shape[0]
    taps = jnp.concatenate([sweight[...], jnp.zeros((SUB, cd), F32)], axis=0)
    shift = 1
    while shift < SUB:
        taps = jnp.where((first & shift) != 0, pltpu.roll(taps, shift, 0), taps)
        shift *= 2
    group = jnp.broadcast_to(first // SUB - me_c * (sd // SUB), (SUB, cd))
    blank = jnp.zeros((SUB, cd), F32)
    for block in range(sd // LANES + 1):
        parts = []
        for g in range(LANES // SUB):
            if block < sd // LANES:
                number = block * (LANES // SUB) + g
            elif g < HS // SUB:
                number = sd // SUB + g
            elif g >= (LANES - HS) // SUB:
                number = g - LANES // SUB
            else:
                parts.append(blank)
                continue
            part = blank
            for m in range(support // SUB + 1):
                part = jnp.where(group == number - m, taps[m * SUB : (m + 1) * SUB], part)
            parts.append(part)
        head, rest = split(jnp.concatenate(parts, axis=0).T)
        space_head[:, block * LANES : (block + 1) * LANES] = head.astype(BF16)
        space_rest[:, block * LANES : (block + 1) * LANES] = rest.astype(BF16)

    for i, (dt, dc) in enumerate(DIRS):
        @pl.when(there(-dt, -dc))
        def _(i=i, dt=dt, dc=dc):
            forward(i, dt, dc).wait_recv()

    lane = lax.broadcasted_iota(jnp.int32, (rows, LANES), 1)
    edge = jnp.where(lane < HS, high[...].reshape(rows, LANES), jnp.where(lane >= LANES - HS, low[...].reshape(rows, LANES), 0.0))
    head, rest = split(jnp.concatenate([own[...].reshape(rows, sd), edge], axis=1))
    coef = jnp.concatenate([head, rest], axis=0).astype(BF16)
    nt_dims = (((1,), (1,)), ((), ()))
    spatial = lax.dot_general(space_head[...], coef, nt_dims, preferred_element_type=F32)
    spatial = spatial + lax.dot_general(space_rest[...], coef, nt_dims, preferred_element_type=F32)
    spatial = spatial + pltpu.roll(spatial, rows, 1)
    head, rest = split(spatial)
    wide = lax.broadcasted_iota(jnp.int32, (cd, 2 * rows), 1)
    spatial = jnp.where(wide < rows, head, rest)

    lane = lax.broadcasted_iota(jnp.int32, (CHUNK, 2 * rows), 1)
    which = lane % SUB
    for i in range(chunks):
        chunk_loads[i][0].wait()
        chunk_loads[i][1].wait()
        part = slice(i * CHUNK, (i + 1) * CHUNK)
        fields = []
        for n in range(2 * covs):
            picked = jnp.where(which == n, spatial[part], 0.0).astype(BF16)
            fields.append(bf16_dot(jnp.concatenate([picked, picked], axis=1), time_rows[...]))
        predictor = covar[0, part, :] * fields[0]
        tangent_pred = covar[0, part, :] * fields[covs]
        for k in range(1, covs):
            predictor = predictor + covar[k, part, :] * fields[k]
            tangent_pred = tangent_pred + covar[k, part, :] * fields[covs + k]
        rates = jnp.exp(predictor)
        factors = (rates * tangent_pred, counts[part, :].astype(F32) - rates)
        total = jnp.zeros((CHUNK, 2 * rows), F32)
        for n in range(2 * covs):
            head, rest = split(covar[n % covs, part, :] * factors[n // covs])
            value = bf16_dot(head.astype(BF16), time_cols[...]) + bf16_dot(rest.astype(BF16), time_cols[...])
            total = jnp.where(which == n, value, total)
        total = total + pltpu.roll(total, rows, 1)
        head, rest = split(total)
        back[:, part] = jnp.where(lane < rows, head, rest).T.astype(BF16)

    result = bf16_dot(back[...], space_head[...]) + bf16_dot(back[...], space_rest[...])
    result = (result[:rows] + result[rows:]).reshape(te, SUB, sd + LANES)
    res_own[...] = result[:, :, :sd]
    res_edge[...] = result[:, :, sd:]

    def backward(i, dt, dc):
        src_t = {0: pl.ds(0, td), 1: pl.ds(td + HT, HT), -1: pl.ds(td, HT)}[dt]
        src = res_edge if dc else res_own
        return pltpu.make_async_remote_copy(
            src_ref=src.at[src_t], dst_ref=got[i],
            send_sem=back_send.at[i], recv_sem=back_recv.at[i], device_id=device(dt, dc), device_id_type=MESH,
        )

    for i, (dt, dc) in enumerate(DIRS):
        @pl.when(there(dt, dc))
        def _(i=i, dt=dt, dc=dc):
            forward(i, dt, dc).wait_send()
            backward(i, dt, dc).start()
    for i, (dt, dc) in enumerate(DIRS):
        @pl.when(there(-dt, -dc))
        def _(i=i, dt=dt, dc=dc):
            backward(i, dt, dc).wait_recv()

    lane = lax.broadcasted_iota(jnp.int32, (1, 1, LANES), 2)
    sums = [[res_own[t : t + 1, :, b * LANES : (b + 1) * LANES] for b in range(sd // LANES)] for t in range(td)]
    for i, (dt, dc) in enumerate(DIRS):
        start = td - HT if dt < 0 else 0
        for t in range(got[i].shape[0]):
            value = got[i][t : t + 1]
            if dc == 0:
                for b in range(sd // LANES):
                    sums[start + t][b] += value[:, :, b * LANES : (b + 1) * LANES]
            elif dc > 0:
                sums[start + t][0] += jnp.where(lane < HS, value, 0.0)
            else:
                sums[start + t][-1] += jnp.where(lane >= LANES - HS, value, 0.0)
    total = jnp.concatenate([jnp.concatenate(row, axis=2) for row in sums], axis=0)
    for p in range(2):
        scale = F32((sweight.shape[0] if p == 0 else 1) * (hd // td))
        for k in range(covs):
            out_ref[p, k] = total[:, p * covs + k, :] / scale

    for i, (dt, dc) in enumerate(DIRS):
        @pl.when(there(dt, dc))
        def _(i=i, dt=dt, dc=dc):
            backward(i, dt, dc).wait_send()


def body(nt, nc, theta, tangent, covariates, counts, sfirst, sweight, tfirst, tweight):
    covs, sd, td = theta.shape
    cd, hd = counts.shape
    te = td + 2 * HT
    operands = (
        theta.transpose(0, 2, 1), tangent.transpose(0, 2, 1), covariates, counts,
        sfirst.reshape(1, cd), sweight, tfirst.reshape(1, hd), tweight,
    )
    got = [
        pltpu.VMEM((HT if dt else td, SUB, LANES if dc else sd), F32) for dt, dc in DIRS
    ]
    dirs = len(DIRS)
    out = pl.pallas_call(
        functools.partial(kernel, nt, nc),
        out_shape=jax.ShapeDtypeStruct((2, covs, td, sd), F32),
        in_specs=[pl.BlockSpec(memory_space=pltpu.HBM)] * len(operands),
        out_specs=pl.BlockSpec(memory_space=pltpu.VMEM),
        scratch_shapes=[pltpu.VMEM(x.shape, x.dtype) for x in operands]
        + [
            pltpu.VMEM((te, SUB, sd), F32),
            pltpu.VMEM((te, SUB, LANES), F32),
            pltpu.VMEM((te, SUB, LANES), F32),
            pltpu.VMEM((cd, sd + LANES), BF16),
            pltpu.VMEM((cd, sd + LANES), BF16),
            pltpu.VMEM((4 * te * SUB, hd), BF16),
            pltpu.VMEM((hd, 2 * te * SUB), BF16),
            pltpu.VMEM((2 * te * SUB, cd), BF16),
            pltpu.VMEM((te, SUB, sd), F32),
            pltpu.VMEM((te, SUB, LANES), F32),
            got,
            pltpu.SemaphoreType.DMA((6,)),
            pltpu.SemaphoreType.DMA((2, cd // CHUNK)),
            pltpu.SemaphoreType.DMA((dirs,)),
            pltpu.SemaphoreType.DMA((dirs,)),
            pltpu.SemaphoreType.DMA((dirs,)),
            pltpu.SemaphoreType.DMA((dirs,)),
        ],
        compiler_params=pltpu.CompilerParams(
            collective_id=0, has_side_effects=True, vmem_limit_bytes=60 * 1024 * 1024
        ),
        name="hessian_product",
    )(*operands)
    out = out.transpose(0, 1, 3, 2)
    return out[0], out[1]


def solution(mesh):
    return jax.shard_map(
        functools.partial(body, mesh.shape["tm"], mesh.shape["cell"]),
        mesh=mesh,
        in_specs=(
            P(None, "cell", "tm"),
            P(None, "cell", "tm"),
            P(None, "cell", "tm"),
            P("cell", "tm"),
            P("cell"),
            P(None, "cell"),
            P("tm"),
            P(None, "tm"),
        ),
        out_specs=(P(None, "cell", "tm"), P(None, "cell", "tm")),
        check_vma=False,
    )
```

time: 56.6 us -> 19.2 us (0.34)
  the two profiles are of different devices: /device:TPU:11 before, /device:TPU:1 now
where the time goes in v1:
time: 19.2 us; the launch traced here: 18.9 us
  Pallas kernels  16.9 us (88%)
  local copies, waits for them, and re-layouts  1.33 us (7%)
  between operations  0.64 us (3%)
    pallas_call x1, Pallas kernels, body(): pl.pallas_call(functools.partial(kernel, nt, nc), out_shape=jax.ShapeDtyp...  16.9 us
    squeeze x1, local copies, waits for them, and re-layouts, body(): return (out[0], out[1])  1.33 us

profile of v1, /device:TPU:1, one launch (start us, length us, event | category | flops | bytes accessed | tf_op | source)
XLA Modules:
  0.0 18.9 jit_solution(13974641259145214210)
XLA Ops:
  0.6 16.9 %hessian_product.1 = f32[2,3,4,256]{3,2,1,0:T(4,128)} custom-call(f32[3,4,256]{2,1,0:T(4,128)} %bitcast.10, f32[3,4,256]{2,1,0:T(4,128)} %bitcast.11, f32[3,512,512]{2,1,0:T(8,128)} %covar_h.1, s32[512,512]{1,0:T(8,128)} %counts_h.1, s32[1,512]{1,0:T(1,128)} %bitcast.12, f32[16,512]{1,0:T(8,128)} %sweight_h.1, s32[1,512]{1,0:T(1,128)} %bitcast.13, ...), custom_call_target="tpu_custom_call" | custom-call | tf_op jit(solution)/shard_map/hessian_product/pallas_call | solution.py:252
  17.6 1.3 %slice_bitcast_fusion = (f32[3,256,4]{1,2,0:T(4,128)}, f32[3,256,4]{1,2,0:T(4,128)}) fusion(f32[2,3,256,4]{2,3,1,0:T(4,128)} %bitcast.9), kind=kLoop, calls=%fused_computation | loop fusion | bytes 49152 | tf_op jit(solution)/shard_map/squeeze | solution.py:283

commit v2 on v1

--- a/solution.py
+++ b/solution.py
@@ -12,6 +12,8 @@
 LANES = 128
 SUB = 8
 CHUNK = 128
+STRIP = 16
+STRIP_COLS = 256
 MESH = pl.DeviceIdType.MESH
 DIRS = [(dt, dc) for dt in (1, -1, 0) for dc in (0, 1, -1) if (dt, dc) != (0, 0)]
 F32 = jnp.float32
@@ -19,6 +21,11 @@
 
 
 def split(value):
+    head = value.astype(BF16)
+    return head, (value - head.astype(F32)).astype(BF16)
+
+
+def split_wide(value):
     head = value.astype(BF16).astype(F32)
     return head, value - head
 
@@ -30,7 +37,7 @@
 def kernel(
     nt, nc, theta_h, tangent_h, covar_h, counts_h, sfirst_h, sweight_h, tfirst_h, tweight_h, out_ref,
     theta, tangent, covar, counts, sfirst, sweight, tfirst, tweight,
-    own, low, high, space_head, space_rest, time_rows, time_cols, back,
+    own, low, high, space_head, space_rest, time_rows, time_cols, spatial, fields, weighted, back,
     res_own, res_edge, got, load_sem, chunk_sem, send_sem, recv_sem, back_send, back_recv,
 ):
     covs, td, sd = theta.shape
@@ -40,12 +47,36 @@
     chunks = cd // CHUNK
     me_t, me_c = lax.axis_index("tm"), lax.axis_index("cell")
 
-    loads = []
-    for i, (src, dst) in enumerate(
-        [(theta_h, theta), (tangent_h, tangent), (tfirst_h, tfirst), (tweight_h, tweight), (sfirst_h, sfirst), (sweight_h, sweight)]
-    ):
-        loads.append(pltpu.make_async_copy(src, dst, load_sem.at[i]))
-        loads[-1].start()
+    loads = [
+        pltpu.make_async_copy(src, dst, load_sem.at[i])
+        for i, (src, dst) in enumerate(
+            [(theta_h, theta), (tangent_h, tangent), (tfirst_h, tfirst), (tweight_h, tweight), (sfirst_h, sfirst), (sweight_h, sweight)]
+        )
+    ]
+    loads[0].start()
+    loads[1].start()
+
+    def there(dt, dc):
+        inside = me_t >= 0
+        if dt:
+            inside = jnp.logical_and(inside, (me_t < nt - 1) if dt > 0 else (me_t > 0))
+        if dc:
+            inside = jnp.logical_and(inside, (me_c < nc - 1) if dc > 0 else (me_c > 0))
+        return inside
+
+    def device(dt, dc):
+        return {"tm": me_t + dt, "cell": me_c + dc}
+
+    for ref in [own, low, high] + got:
+        ref[...] = jnp.zeros(ref.shape, F32)
+    barrier = pltpu.get_barrier_semaphore()
+    for dt, dc in DIRS:
+        @pl.when(there(dt, dc))
+        def _(dt=dt, dc=dc):
+            pl.semaphore_signal(barrier, inc=1, device_id=device(dt, dc), device_id_type=MESH)
+
+    for copy in loads[2:]:
+        copy.start()
     chunk_loads = []
     for i in range(chunks):
         part = pl.ds(i * CHUNK, CHUNK)
@@ -57,44 +88,11 @@
             copy.start()
         chunk_loads.append(pair)
 
-    def there(dt, dc):
-        inside = me_t >= 0
-        if dt:
-            inside = jnp.logical_and(inside, (me_t < nt - 1) if dt > 0 else (me_t > 0))
-        if dc:
-            inside = jnp.logical_and(inside, (me_c < nc - 1) if dc > 0 else (me_c > 0))
-        return inside
-
-    def device(dt, dc):
-        return {"tm": me_t + dt, "cell": me_c + dc}
-
-    for ref in [own, low, high] + got:
-        ref[...] = jnp.zeros(ref.shape, F32)
-    barrier = pltpu.get_barrier_semaphore()
-    for dt, dc in DIRS:
-        @pl.when(there(dt, dc))
-        def _(dt=dt, dc=dc):
-            pl.semaphore_signal(barrier, inc=1, device_id=device(dt, dc), device_id_type=MESH)
-
     loads[0].wait()
     loads[1].wait()
     for p, ref in enumerate((theta, tangent)):
         for k in range(covs):
             own[0:td, p * covs + k, :] = ref[k]
-
-    loads[2].wait()
-    loads[3].wait()
-    index = lax.broadcasted_iota(jnp.int32, (rows, hd), 0) // SUB
-    place = jnp.where(index < td, index, jnp.where(index < td + HT, index - (td + HT), index - HT)) + me_t * td
-    diffs = place - tfirst[...]
-    basis = jnp.zeros((rows, hd), F32)
-    for j in range(tweight.shape[0]):
-        basis = jnp.where(diffs == j, tweight[j : j + 1, :], basis)
-    head, rest = split(basis)
-    both = jnp.concatenate([head, rest], axis=0)
-    time_cols[...] = both.T.astype(BF16)
-    head, rest = head.astype(BF16), rest.astype(BF16)
-    time_rows[...] = jnp.concatenate([head, head, rest, rest], axis=0)
 
     beside_t = (me_t > 0).astype(jnp.int32) + (me_t < nt - 1).astype(jnp.int32)
     beside_c = (me_c > 0).astype(jnp.int32) + (me_c < nc - 1).astype(jnp.int32)
@@ -114,6 +112,20 @@
         @pl.when(there(dt, dc))
         def _(i=i, dt=dt, dc=dc):
             forward(i, dt, dc).start()
+
+    loads[2].wait()
+    loads[3].wait()
+    index = lax.broadcasted_iota(jnp.int32, (rows, hd), 0) // SUB
+    place = jnp.where(index < td, index, jnp.where(index < td + HT, index - (td + HT), index - HT)) + me_t * td
+    diffs = place - tfirst[...]
+    basis = jnp.zeros((rows, hd), F32)
+    for j in range(tweight.shape[0]):
+        basis = jnp.where(diffs == j, tweight[j : j + 1, :], basis)
+    head, rest = split_wide(basis)
+    turned = jnp.concatenate([head, rest], axis=0).T.astype(BF16)
+    time_cols[...] = jnp.concatenate([turned, turned], axis=0)
+    head, rest = head.astype(BF16), rest.astype(BF16)
+    time_rows[...] = jnp.concatenate([head, head, rest, rest], axis=0)
 
     loads[4].wait()
     loads[5].wait()
@@ -143,8 +155,8 @@
                 part = jnp.where(group == number - m, taps[m * SUB : (m + 1) * SUB], part)
             parts.append(part)
         head, rest = split(jnp.concatenate(parts, axis=0).T)
-        space_head[:, block * LANES : (block + 1) * LANES] = head.astype(BF16)
-        space_rest[:, block * LANES : (block + 1) * LANES] = rest.astype(BF16)
+        space_head[:, block * LANES : (block + 1) * LANES] = head
+        space_rest[:, block * LANES : (block + 1) * LANES] = rest
 
     for i, (dt, dc) in enumerate(DIRS):
         @pl.when(there(-dt, -dc))
@@ -154,45 +166,65 @@
     lane = lax.broadcasted_iota(jnp.int32, (rows, LANES), 1)
     edge = jnp.where(lane < HS, high[...].reshape(rows, LANES), jnp.where(lane >= LANES - HS, low[...].reshape(rows, LANES), 0.0))
     head, rest = split(jnp.concatenate([own[...].reshape(rows, sd), edge], axis=1))
-    coef = jnp.concatenate([head, rest], axis=0).astype(BF16)
+    coef = jnp.concatenate([head, rest], axis=0)
     nt_dims = (((1,), (1,)), ((), ()))
-    spatial = lax.dot_general(space_head[...], coef, nt_dims, preferred_element_type=F32)
-    spatial = spatial + lax.dot_general(space_rest[...], coef, nt_dims, preferred_element_type=F32)
-    spatial = spatial + pltpu.roll(spatial, rows, 1)
-    head, rest = split(spatial)
+    value = lax.dot_general(space_head[...], coef, nt_dims, preferred_element_type=F32)
+    value = value + lax.dot_general(space_rest[...], coef, nt_dims, preferred_element_type=F32)
+    value = value + pltpu.roll(value, rows, 1)
+    head, rest = split_wide(value)
     wide = lax.broadcasted_iota(jnp.int32, (cd, 2 * rows), 1)
-    spatial = jnp.where(wide < rows, head, rest)
+    spatial[...] = jnp.where(wide < rows, head, rest)
 
     lane = lax.broadcasted_iota(jnp.int32, (CHUNK, 2 * rows), 1)
     which = lane % SUB
+
+    def fields_of(i):
+        value = spatial[i * CHUNK : (i + 1) * CHUNK, :]
+        picked = [jnp.where(which == n, value, 0.0).astype(BF16) for n in range(2 * covs)]
+        picked = jnp.concatenate(picked, axis=0)
+        fields[i % 2] = bf16_dot(jnp.concatenate([picked, picked], axis=1), time_rows[...])
+
+    def weigh(i):
+        for r in range(0, CHUNK, STRIP):
+            for c in range(0, hd, STRIP_COLS):
+                cells = slice(i * CHUNK + r, i * CHUNK + r + STRIP)
+                hours = slice(c, c + STRIP_COLS)
+                cov = [covar[k, cells, hours] for k in range(covs)]
+
+                def field(n):
+                    return fields[i % 2, n * CHUNK + r : n * CHUNK + r + STRIP, hours]
+
+                predictor = cov[0] * field(0)
+                tangent_pred = cov[0] * field(covs)
+                for k in range(1, covs):
+                    predictor = predictor + cov[k] * field(k)
+                    tangent_pred = tangent_pred + cov[k] * field(covs + k)
+                rates = jnp.exp(predictor)
+                factors = (rates * tangent_pred, counts[cells, hours].astype(F32) - rates)
+                for n in range(2 * covs):
+                    head, rest = split(cov[n % covs] * factors[n // covs])
+                    place = slice(n * CHUNK + r, n * CHUNK + r + STRIP)
+                    weighted[i % 2, place, c : c + STRIP_COLS] = head
+                    weighted[i % 2, place, hd + c : hd + c + STRIP_COLS] = rest
+
+    def sums_of(i):
+        value = bf16_dot(weighted[i % 2], time_cols[...])
+        total = value[:CHUNK]
+        for n in range(1, 2 * covs):
+            total = jnp.where(which == n, value[n * CHUNK : (n + 1) * CHUNK], total)
+        total = jnp.where(which < 2 * covs, total, 0.0)
+        total = total + pltpu.roll(total, rows, 1)
+        head, rest = split_wide(total)
+        back[:, i * CHUNK : (i + 1) * CHUNK] = jnp.where(lane < rows, head, rest).T.astype(BF16)
+
+    fields_of(0)
     for i in range(chunks):
         chunk_loads[i][0].wait()
         chunk_loads[i][1].wait()
-        part = slice(i * CHUNK, (i + 1) * CHUNK)
-        fields = []
-        for n in range(2 * covs):
-            picked = jnp.where(which == n, spatial[part], 0.0).astype(BF16)
-            fields.append(bf16_dot(jnp.concatenate([picked, picked], axis=1), time_rows[...]))
-        predictor = covar[0, part, :] * fields[0]
-        tangent_pred = covar[0, part, :] * fields[covs]
-        for k in range(1, covs):
-            predictor = predictor + covar[k, part, :] * fields[k]
-            tangent_pred = tangent_pred + covar[k, part, :] * fields[covs + k]
-        rates = jnp.exp(predictor)
-        factors = (rates * tangent_pred, counts[part, :].astype(F32) - rates)
-        total = jnp.zeros((CHUNK, 2 * rows), F32)
-        for n in range(2 * covs):
-            head, rest = split(covar[n % covs, part, :] * factors[n // covs])
-            value = bf16_dot(head.astype(BF16), time_cols[...]) + bf16_dot(rest.astype(BF16), time_cols[...])
-            total = jnp.where(which == n, value, total)
-        total = total + pltpu.roll(total, rows, 1)
-        head, rest = split(total)
-        back[:, part] = jnp.where(lane < rows, head, rest).T.astype(BF16)
-
-    result = bf16_dot(back[...], space_head[...]) + bf16_dot(back[...], space_rest[...])
-    result = (result[:rows] + result[rows:]).reshape(te, SUB, sd + LANES)
-    res_own[...] = result[:, :, :sd]
-    res_edge[...] = result[:, :, sd:]
+        if i + 1 < chunks:
+            fields_of(i + 1)
+        weigh(i)
+        sums_of(i)
 
     def backward(i, dt, dc):
         src_t = {0: pl.ds(0, td), 1: pl.ds(td + HT, HT), -1: pl.ds(td, HT)}[dt]
@@ -202,11 +234,16 @@
             send_sem=back_send.at[i], recv_sem=back_recv.at[i], device_id=device(dt, dc), device_id_type=MESH,
         )
 
-    for i, (dt, dc) in enumerate(DIRS):
-        @pl.when(there(dt, dc))
-        def _(i=i, dt=dt, dc=dc):
-            forward(i, dt, dc).wait_send()
-            backward(i, dt, dc).start()
+    for edges in (True, False):
+        columns = slice(sd, sd + LANES) if edges else slice(0, sd)
+        result = bf16_dot(back[...], space_head[:, columns]) + bf16_dot(back[...], space_rest[:, columns])
+        result = result[:rows] + result[rows:]
+        (res_edge if edges else res_own)[...] = result.reshape(te, SUB, LANES if edges else sd)
+        for i, (dt, dc) in enumerate(DIRS):
+            if (dc != 0) == edges:
+                @pl.when(there(dt, dc))
+                def _(i=i, dt=dt, dc=dc):
+                    backward(i, dt, dc).start()
     for i, (dt, dc) in enumerate(DIRS):
         @pl.when(there(-dt, -dc))
         def _(i=i, dt=dt, dc=dc):
@@ -234,6 +271,7 @@
     for i, (dt, dc) in enumerate(DIRS):
         @pl.when(there(dt, dc))
         def _(i=i, dt=dt, dc=dc):
+            forward(i, dt, dc).wait_send()
             backward(i, dt, dc).wait_send()
 
 
@@ -262,7 +300,10 @@
             pltpu.VMEM((cd, sd + LANES), BF16),
             pltpu.VMEM((cd, sd + LANES), BF16),
             pltpu.VMEM((4 * te * SUB, hd), BF16),
-            pltpu.VMEM((hd, 2 * te * SUB), BF16),
+            pltpu.VMEM((2 * hd, 2 * te * SUB), BF16),
+            pltpu.VMEM((cd, 2 * te * SUB), F32),
+            pltpu.VMEM((2, 2 * covs * CHUNK, hd), F32),
+            pltpu.VMEM((2, 2 * covs * CHUNK, 2 * hd), BF16),
             pltpu.VMEM((2 * te * SUB, cd), BF16),
             pltpu.VMEM((te, SUB, sd), F32),
             pltpu.VMEM((te, SUB, LANES), F32),

time: 19.2 us -> 20.3 us (1.057)
  Pallas kernels: 16.9 us -> 18 us
    pallas_call x1, Pallas kernels: 16.9 us -> 18 us  [body(): pl.pallas_call(functools.partial(kernel, nt, nc), out_shape=jax.ShapeDtyp...]
where the time goes in v2:
time: 20.3 us; the launch traced here: 20 us
  Pallas kernels  18 us (89%)
  local copies, waits for them, and re-layouts  1.33 us (7%)
  between operations  0.64 us (3%)
    pallas_call x1, Pallas kernels, body(): pl.pallas_call(functools.partial(kernel, nt, nc), out_shape=jax.ShapeDtyp...  18 us
    squeeze x1, local copies, waits for them, and re-layouts, body(): return (out[0], out[1])  1.33 us

profile of v2, /device:TPU:1, one launch (start us, length us, event | category | flops | bytes accessed | tf_op | source)
XLA Modules:
  0.0 20.0 jit_solution(11331267054387777620)
XLA Ops:
  0.6 18.0 %hessian_product.1 = f32[2,3,4,256]{3,2,1,0:T(4,128)} custom-call(f32[3,4,256]{2,1,0:T(4,128)} %bitcast.10, f32[3,4,256]{2,1,0:T(4,128)} %bitcast.11, f32[3,512,512]{2,1,0:T(8,128)} %covar_h.1, s32[512,512]{1,0:T(8,128)} %counts_h.1, s32[1,512]{1,0:T(1,128)} %bitcast.12, f32[16,512]{1,0:T(8,128)} %sweight_h.1, s32[1,512]{1,0:T(1,128)} %bitcast.13, ...), custom_call_target="tpu_custom_call" | custom-call | tf_op jit(solution)/shard_map/hessian_product/pallas_call | solution.py:290
  18.6 1.3 %slice_bitcast_fusion = (f32[3,256,4]{1,2,0:T(4,128)}, f32[3,256,4]{1,2,0:T(4,128)}) fusion(f32[2,3,256,4]{2,3,1,0:T(4,128)} %bitcast.9), kind=kLoop, calls=%fused_computation | loop fusion | bytes 49152 | tf_op jit(solution)/shard_map/squeeze | solution.py:324

commit v3 on v2

--- a/solution.py
+++ b/solution.py
@@ -12,8 +12,6 @@
 LANES = 128
 SUB = 8
 CHUNK = 128
-STRIP = 16
-STRIP_COLS = 256
 MESH = pl.DeviceIdType.MESH
 DIRS = [(dt, dc) for dt in (1, -1, 0) for dc in (0, 1, -1) if (dt, dc) != (0, 0)]
 F32 = jnp.float32
@@ -37,14 +35,13 @@
 def kernel(
     nt, nc, theta_h, tangent_h, covar_h, counts_h, sfirst_h, sweight_h, tfirst_h, tweight_h, out_ref,
     theta, tangent, covar, counts, sfirst, sweight, tfirst, tweight,
-    own, low, high, space_head, space_rest, time_rows, time_cols, spatial, fields, weighted, back,
-    res_own, res_edge, got, load_sem, chunk_sem, send_sem, recv_sem, back_send, back_recv,
+    own, low, high, space_head, space_rest, time_rows, time_cols, back,
+    res_own, res_edge, got, load_sem, send_sem, recv_sem, back_send, back_recv,
 ):
     covs, td, sd = theta.shape
     cd, hd = counts.shape
     te = td + 2 * HT
     rows = te * SUB
-    chunks = cd // CHUNK
     me_t, me_c = lax.axis_index("tm"), lax.axis_index("cell")
 
     loads = [
@@ -77,16 +74,12 @@
 
     for copy in loads[2:]:
         copy.start()
-    chunk_loads = []
-    for i in range(chunks):
-        part = pl.ds(i * CHUNK, CHUNK)
-        pair = (
-            pltpu.make_async_copy(covar_h.at[:, part], covar.at[:, part], chunk_sem.at[0, i]),
-            pltpu.make_async_copy(counts_h.at[part], counts.at[part], chunk_sem.at[1, i]),
-        )
-        for copy in pair:
-            copy.start()
-        chunk_loads.append(pair)
+    chunk_loads = [
+        pltpu.make_async_copy(covar_h, covar, load_sem.at[6]),
+        pltpu.make_async_copy(counts_h, counts, load_sem.at[7]),
+    ]
+    for copy in chunk_loads:
+        copy.start()
 
     loads[0].wait()
     loads[1].wait()
@@ -123,7 +116,7 @@
         basis = jnp.where(diffs == j, tweight[j : j + 1, :], basis)
     head, rest = split_wide(basis)
     turned = jnp.concatenate([head, rest], axis=0).T.astype(BF16)
-    time_cols[...] = jnp.concatenate([turned, turned], axis=0)
+    time_cols[...] = turned
     head, rest = head.astype(BF16), rest.astype(BF16)
     time_rows[...] = jnp.concatenate([head, head, rest, rest], axis=0)
 
@@ -173,58 +166,33 @@
     value = value + pltpu.roll(value, rows, 1)
     head, rest = split_wide(value)
     wide = lax.broadcasted_iota(jnp.int32, (cd, 2 * rows), 1)
-    spatial[...] = jnp.where(wide < rows, head, rest)
-
+    spatial = jnp.where(wide < rows, head, rest)
+
+    for copy in chunk_loads:
+        copy.wait()
     lane = lax.broadcasted_iota(jnp.int32, (CHUNK, 2 * rows), 1)
     which = lane % SUB
-
-    def fields_of(i):
-        value = spatial[i * CHUNK : (i + 1) * CHUNK, :]
-        picked = [jnp.where(which == n, value, 0.0).astype(BF16) for n in range(2 * covs)]
-        picked = jnp.concatenate(picked, axis=0)
-        fields[i % 2] = bf16_dot(jnp.concatenate([picked, picked], axis=1), time_rows[...])
-
-    def weigh(i):
-        for r in range(0, CHUNK, STRIP):
-            for c in range(0, hd, STRIP_COLS):
-                cells = slice(i * CHUNK + r, i * CHUNK + r + STRIP)
-                hours = slice(c, c + STRIP_COLS)
-                cov = [covar[k, cells, hours] for k in range(covs)]
-
-                def field(n):
-                    return fields[i % 2, n * CHUNK + r : n * CHUNK + r + STRIP, hours]
-
-                predictor = cov[0] * field(0)
-                tangent_pred = cov[0] * field(covs)
-                for k in range(1, covs):
-                    predictor = predictor + cov[k] * field(k)
-                    tangent_pred = tangent_pred + cov[k] * field(covs + k)
-                rates = jnp.exp(predictor)
-                factors = (rates * tangent_pred, counts[cells, hours].astype(F32) - rates)
-                for n in range(2 * covs):
-                    head, rest = split(cov[n % covs] * factors[n // covs])
-                    place = slice(n * CHUNK + r, n * CHUNK + r + STRIP)
-                    weighted[i % 2, place, c : c + STRIP_COLS] = head
-                    weighted[i % 2, place, hd + c : hd + c + STRIP_COLS] = rest
-
-    def sums_of(i):
-        value = bf16_dot(weighted[i % 2], time_cols[...])
-        total = value[:CHUNK]
-        for n in range(1, 2 * covs):
-            total = jnp.where(which == n, value[n * CHUNK : (n + 1) * CHUNK], total)
-        total = jnp.where(which < 2 * covs, total, 0.0)
+    for start in range(0, cd, CHUNK):
+        part = slice(start, start + CHUNK)
+        fields = []
+        for n in range(2 * covs):
+            picked = jnp.where(which == n, spatial[part], 0.0).astype(BF16)
+            fields.append(bf16_dot(jnp.concatenate([picked, picked], axis=1), time_rows[...]))
+        predictor = covar[0, part, :] * fields[0]
+        tangent_pred = covar[0, part, :] * fields[covs]
+        for k in range(1, covs):
+            predictor = predictor + covar[k, part, :] * fields[k]
+            tangent_pred = tangent_pred + covar[k, part, :] * fields[covs + k]
+        rates = jnp.exp(predictor)
+        factors = (rates * tangent_pred, counts[part, :].astype(F32) - rates)
+        total = jnp.zeros((CHUNK, 2 * rows), F32)
+        for n in range(2 * covs):
+            head, rest = split(covar[n % covs, part, :] * factors[n // covs])
+            value = bf16_dot(head, time_cols[...]) + bf16_dot(rest, time_cols[...])
+            total = jnp.where(which == n, value, total)
         total = total + pltpu.roll(total, rows, 1)
         head, rest = split_wide(total)
-        back[:, i * CHUNK : (i + 1) * CHUNK] = jnp.where(lane < rows, head, rest).T.astype(BF16)
-
-    fields_of(0)
-    for i in range(chunks):
-        chunk_loads[i][0].wait()
-        chunk_loads[i][1].wait()
-        if i + 1 < chunks:
-            fields_of(i + 1)
-        weigh(i)
-        sums_of(i)
+        back[:, part] = jnp.where(lane < rows, head, rest).T.astype(BF16)
 
     def backward(i, dt, dc):
         src_t = {0: pl.ds(0, td), 1: pl.ds(td + HT, HT), -1: pl.ds(td, HT)}[dt]
@@ -300,16 +268,12 @@
             pltpu.VMEM((cd, sd + LANES), BF16),
             pltpu.VMEM((cd, sd + LANES), BF16),
             pltpu.VMEM((4 * te * SUB, hd), BF16),
-            pltpu.VMEM((2 * hd, 2 * te * SUB), BF16),
-            pltpu.VMEM((cd, 2 * te * SUB), F32),
-            pltpu.VMEM((2, 2 * covs * CHUNK, hd), F32),
-            pltpu.VMEM((2, 2 * covs * CHUNK, 2 * hd), BF16),
+            pltpu.VMEM((hd, 2 * te * SUB), BF16),
             pltpu.VMEM((2 * te * SUB, cd), BF16),
             pltpu.VMEM((te, SUB, sd), F32),
             pltpu.VMEM((te, SUB, LANES), F32),
             got,
-            pltpu.SemaphoreType.DMA((6,)),
-            pltpu.SemaphoreType.DMA((2, cd // CHUNK)),
+            pltpu.SemaphoreType.DMA((8,)),
             pltpu.SemaphoreType.DMA((dirs,)),
             pltpu.SemaphoreType.DMA((dirs,)),
             pltpu.SemaphoreType.DMA((dirs,)),

time: 20.3 us -> 18 us (0.89)
  Pallas kernels: 18 us -> 15.7 us
    pallas_call x1, Pallas kernels: 18 us -> 15.7 us  [body(): pl.pallas_call(functools.partial(kernel, nt, nc), out_shape=jax.ShapeDtyp...]
where the time goes in v3:
time: 18 us; the launch traced here: 17.7 us
  Pallas kernels  15.7 us (87%)
  local copies, waits for them, and re-layouts  1.33 us (7%)
  between operations  0.64 us (4%)
    pallas_call x1, Pallas kernels, body(): pl.pallas_call(functools.partial(kernel, nt, nc), out_shape=jax.ShapeDtyp...  15.7 us
    squeeze x1, local copies, waits for them, and re-layouts, body(): return (out[0], out[1])  1.33 us

profile of v3, /device:TPU:1, one launch (start us, length us, event | category | flops | bytes accessed | tf_op | source)
XLA Modules:
  0.0 17.7 jit_solution(12485087283693880063)
XLA Ops:
  0.6 15.7 %hessian_product.1 = f32[2,3,4,256]{3,2,1,0:T(4,128)} custom-call(f32[3,4,256]{2,1,0:T(4,128)} %bitcast.10, f32[3,4,256]{2,1,0:T(4,128)} %bitcast.11, f32[3,512,512]{2,1,0:T(8,128)} %covar_h.1, s32[512,512]{1,0:T(8,128)} %counts_h.1, s32[1,512]{1,0:T(1,128)} %bitcast.12, f32[16,512]{1,0:T(8,128)} %sweight_h.1, s32[1,512]{1,0:T(1,128)} %bitcast.13, ...), custom_call_target="tpu_custom_call" | custom-call | tf_op jit(solution)/shard_map/hessian_product/pallas_call | solution.py:258
  16.4 1.3 %slice_bitcast_fusion = (f32[3,256,4]{1,2,0:T(4,128)}, f32[3,256,4]{1,2,0:T(4,128)}) fusion(f32[2,3,256,4]{2,3,1,0:T(4,128)} %bitcast.9), kind=kLoop, calls=%fused_computation | loop fusion | bytes 49152 | tf_op jit(solution)/shard_map/squeeze | solution.py:288

commit v4 on v3

--- a/solution.py
+++ b/solution.py
@@ -11,7 +11,7 @@
 HT = 2
 LANES = 128
 SUB = 8
-CHUNK = 128
+CHUNK = 256
 MESH = pl.DeviceIdType.MESH
 DIRS = [(dt, dc) for dt in (1, -1, 0) for dc in (0, 1, -1) if (dt, dc) != (0, 0)]
 F32 = jnp.float32
@@ -35,7 +35,7 @@
 def kernel(
     nt, nc, theta_h, tangent_h, covar_h, counts_h, sfirst_h, sweight_h, tfirst_h, tweight_h, out_ref,
     theta, tangent, covar, counts, sfirst, sweight, tfirst, tweight,
-    own, low, high, space_head, space_rest, time_rows, time_cols, back,
+    own, low, high, space, time_rows, time_cols, back,
     res_own, res_edge, got, load_sem, send_sem, recv_sem, back_send, back_recv,
 ):
     covs, td, sd = theta.shape
@@ -148,8 +148,8 @@
                 part = jnp.where(group == number - m, taps[m * SUB : (m + 1) * SUB], part)
             parts.append(part)
         head, rest = split(jnp.concatenate(parts, axis=0).T)
-        space_head[:, block * LANES : (block + 1) * LANES] = head
-        space_rest[:, block * LANES : (block + 1) * LANES] = rest
+        space[:cd, block * LANES : (block + 1) * LANES] = head
+        space[cd:, block * LANES : (block + 1) * LANES] = rest
 
     for i, (dt, dc) in enumerate(DIRS):
         @pl.when(there(-dt, -dc))
@@ -161,8 +161,8 @@
     head, rest = split(jnp.concatenate([own[...].reshape(rows, sd), edge], axis=1))
     coef = jnp.concatenate([head, rest], axis=0)
     nt_dims = (((1,), (1,)), ((), ()))
-    value = lax.dot_general(space_head[...], coef, nt_dims, preferred_element_type=F32)
-    value = value + lax.dot_general(space_rest[...], coef, nt_dims, preferred_element_type=F32)
+    value = lax.dot_general(space[...], coef, nt_dims, preferred_element_type=F32)
+    value = value[:cd] + value[cd:]
     value = value + pltpu.roll(value, rows, 1)
     head, rest = split_wide(value)
     wide = lax.broadcasted_iota(jnp.int32, (cd, 2 * rows), 1)
@@ -188,8 +188,8 @@
         total = jnp.zeros((CHUNK, 2 * rows), F32)
         for n in range(2 * covs):
             head, rest = split(covar[n % covs, part, :] * factors[n // covs])
-            value = bf16_dot(head, time_cols[...]) + bf16_dot(rest, time_cols[...])
-            total = jnp.where(which == n, value, total)
+            value = bf16_dot(jnp.concatenate([head, rest], axis=0), time_cols[...])
+            total = jnp.where(which == n, value[:CHUNK] + value[CHUNK:], total)
         total = total + pltpu.roll(total, rows, 1)
         head, rest = split_wide(total)
         back[:, part] = jnp.where(lane < rows, head, rest).T.astype(BF16)
@@ -204,7 +204,7 @@
 
     for edges in (True, False):
         columns = slice(sd, sd + LANES) if edges else slice(0, sd)
-        result = bf16_dot(back[...], space_head[:, columns]) + bf16_dot(back[...], space_rest[:, columns])
+        result = bf16_dot(jnp.concatenate([back[...], back[...]], axis=1), space[:, columns])
         result = result[:rows] + result[rows:]
         (res_edge if edges else res_own)[...] = result.reshape(te, SUB, LANES if edges else sd)
         for i, (dt, dc) in enumerate(DIRS):
@@ -265,8 +265,7 @@
             pltpu.VMEM((te, SUB, sd), F32),
             pltpu.VMEM((te, SUB, LANES), F32),
             pltpu.VMEM((te, SUB, LANES), F32),
-            pltpu.VMEM((cd, sd + LANES), BF16),
-            pltpu.VMEM((cd, sd + LANES), BF16),
+            pltpu.VMEM((2 * cd, sd + LANES), BF16),
             pltpu.VMEM((4 * te * SUB, hd), BF16),
             pltpu.VMEM((hd, 2 * te * SUB), BF16),
             pltpu.VMEM((2 * te * SUB, cd), BF16),

time: 18 us -> 17.7 us (0.983)
  Pallas kernels: 15.7 us -> 15.4 us
    pallas_call x1, Pallas kernels: 15.7 us -> 15.4 us  [body(): pl.pallas_call(functools.partial(kernel, nt, nc), out_shape=jax.ShapeDtyp...]
where the time goes in v4:
time: 17.7 us; the launch traced here: 17.4 us
  Pallas kernels  15.4 us (87%)
  local copies, waits for them, and re-layouts  1.33 us (8%)
  between operations  0.64 us (4%)
    pallas_call x1, Pallas kernels, body(): pl.pallas_call(functools.partial(kernel, nt, nc), out_shape=jax.ShapeDtyp...  15.4 us
    squeeze x1, local copies, waits for them, and re-layouts, body(): return (out[0], out[1])  1.33 us

profile of v4, /device:TPU:1, one launch (start us, length us, event | category | flops | bytes accessed | tf_op | source)
XLA Modules:
  0.0 17.4 jit_solution(4072268631517992665)
XLA Ops:
  0.6 15.4 %hessian_product.1 = f32[2,3,4,256]{3,2,1,0:T(4,128)} custom-call(f32[3,4,256]{2,1,0:T(4,128)} %bitcast.10, f32[3,4,256]{2,1,0:T(4,128)} %bitcast.11, f32[3,512,512]{2,1,0:T(8,128)} %covar_h.1, s32[512,512]{1,0:T(8,128)} %counts_h.1, s32[1,512]{1,0:T(1,128)} %bitcast.12, f32[16,512]{1,0:T(8,128)} %sweight_h.1, s32[1,512]{1,0:T(1,128)} %bitcast.13, ...), custom_call_target="tpu_custom_call" | custom-call | tf_op jit(solution)/shard_map/hessian_product/pallas_call | solution.py:258
  16.1 1.3 %slice_bitcast_fusion = (f32[3,256,4]{1,2,0:T(4,128)}, f32[3,256,4]{1,2,0:T(4,128)}) fusion(f32[2,3,256,4]{2,3,1,0:T(4,128)} %bitcast.9), kind=kLoop, calls=%fused_computation | loop fusion | bytes 49152 | tf_op jit(solution)/shard_map/squeeze | solution.py:287

commit v5 on v4

--- a/solution.py
+++ b/solution.py
@@ -11,7 +11,7 @@
 HT = 2
 LANES = 128
 SUB = 8
-CHUNK = 256
+CHUNK = 512
 MESH = pl.DeviceIdType.MESH
 DIRS = [(dt, dc) for dt in (1, -1, 0) for dc in (0, 1, -1) if (dt, dc) != (0, 0)]
 F32 = jnp.float32
@@ -108,9 +108,9 @@
 
     loads[2].wait()
     loads[3].wait()
-    index = lax.broadcasted_iota(jnp.int32, (rows, hd), 0) // SUB
+    index = lax.broadcasted_iota(jnp.int32, (rows, LANES), 0) >> (SUB.bit_length() - 1)
     place = jnp.where(index < td, index, jnp.where(index < td + HT, index - (td + HT), index - HT)) + me_t * td
-    diffs = place - tfirst[...]
+    diffs = jnp.concatenate([place] * (hd // LANES), axis=1) - tfirst[...]
     basis = jnp.zeros((rows, hd), F32)
     for j in range(tweight.shape[0]):
         basis = jnp.where(diffs == j, tweight[j : j + 1, :], basis)
@@ -129,7 +129,7 @@
     while shift < SUB:
         taps = jnp.where((first & shift) != 0, pltpu.roll(taps, shift, 0), taps)
         shift *= 2
-    group = jnp.broadcast_to(first // SUB - me_c * (sd // SUB), (SUB, cd))
+    group = jnp.broadcast_to((first >> (SUB.bit_length() - 1)) - me_c * (sd // SUB), (SUB, cd))
     blank = jnp.zeros((SUB, cd), F32)
     for block in range(sd // LANES + 1):
         parts = []
@@ -171,7 +171,7 @@
     for copy in chunk_loads:
         copy.wait()
     lane = lax.broadcasted_iota(jnp.int32, (CHUNK, 2 * rows), 1)
-    which = lane % SUB
+    which = lane & (SUB - 1)
     for start in range(0, cd, CHUNK):
         part = slice(start, start + CHUNK)
         fields = []

time: 17.7 us -> 17.5 us (0.989)
  no operation moved by 1% of the time
where the time goes in v5:
time: 17.5 us; the launch traced here: 17.3 us
  Pallas kernels  15.3 us (87%)
  local copies, waits for them, and re-layouts  1.33 us (8%)
  between operations  0.64 us (4%)
    pallas_call x1, Pallas kernels, body(): pl.pallas_call(functools.partial(kernel, nt, nc), out_shape=jax.ShapeDtyp...  15.3 us
    squeeze x1, local copies, waits for them, and re-layouts, body(): return (out[0], out[1])  1.33 us

profile of v5, /device:TPU:1, one launch (start us, length us, event | category | flops | bytes accessed | tf_op | source)
XLA Modules:
  0.0 17.3 jit_solution(3194940736519632766)
XLA Ops:
  0.6 15.3 %hessian_product.1 = f32[2,3,4,256]{3,2,1,0:T(4,128)} custom-call(f32[3,4,256]{2,1,0:T(4,128)} %bitcast.10, f32[3,4,256]{2,1,0:T(4,128)} %bitcast.11, f32[3,512,512]{2,1,0:T(8,128)} %covar_h.1, s32[512,512]{1,0:T(8,128)} %counts_h.1, s32[1,512]{1,0:T(1,128)} %bitcast.12, f32[16,512]{1,0:T(8,128)} %sweight_h.1, s32[1,512]{1,0:T(1,128)} %bitcast.13, ...), custom_call_target="tpu_custom_call" | custom-call | tf_op jit(solution)/shard_map/hessian_product/pallas_call | solution.py:258
  15.9 1.3 %slice_bitcast_fusion = (f32[3,256,4]{1,2,0:T(4,128)}, f32[3,256,4]{1,2,0:T(4,128)}) fusion(f32[2,3,256,4]{2,3,1,0:T(4,128)} %bitcast.9), kind=kLoop, calls=%fused_computation | loop fusion | bytes 49152 | tf_op jit(solution)/shard_map/squeeze | solution.py:287

commit v6 on v5

--- a/solution.py
+++ b/solution.py
@@ -11,7 +11,7 @@
 HT = 2
 LANES = 128
 SUB = 8
-CHUNK = 512
+CHUNK = 256
 MESH = pl.DeviceIdType.MESH
 DIRS = [(dt, dc) for dt in (1, -1, 0) for dc in (0, 1, -1) if (dt, dc) != (0, 0)]
 F32 = jnp.float32
@@ -170,29 +170,32 @@
 
     for copy in chunk_loads:
         copy.wait()
-    lane = lax.broadcasted_iota(jnp.int32, (CHUNK, 2 * rows), 1)
+    lane = lax.broadcasted_iota(jnp.int32, (cd, 2 * rows), 1)
     which = lane & (SUB - 1)
-    for start in range(0, cd, CHUNK):
+    picked = []
+    for n in range(2 * covs):
+        value = jnp.where(which == n, spatial, 0.0).astype(BF16)
+        picked.append(jnp.concatenate([value, value], axis=1))
+    total = jnp.zeros((cd, 2 * rows), F32)
+    for start in range(0, hd, CHUNK):
         part = slice(start, start + CHUNK)
-        fields = []
+        fields = [bf16_dot(value, time_rows[:, part]) for value in picked]
+        predictor = covar[0, :, part] * fields[0]
+        tangent_pred = covar[0, :, part] * fields[covs]
+        for k in range(1, covs):
+            predictor = predictor + covar[k, :, part] * fields[k]
+            tangent_pred = tangent_pred + covar[k, :, part] * fields[covs + k]
+        rates = jnp.exp(predictor)
+        factors = (rates * tangent_pred, counts[:, part].astype(F32) - rates)
+        sums = jnp.zeros((cd, 2 * rows), F32)
         for n in range(2 * covs):
-            picked = jnp.where(which == n, spatial[part], 0.0).astype(BF16)
-            fields.append(bf16_dot(jnp.concatenate([picked, picked], axis=1), time_rows[...]))
-        predictor = covar[0, part, :] * fields[0]
-        tangent_pred = covar[0, part, :] * fields[covs]
-        for k in range(1, covs):
-            predictor = predictor + covar[k, part, :] * fields[k]
-            tangent_pred = tangent_pred + covar[k, part, :] * fields[covs + k]
-        rates = jnp.exp(predictor)
-        factors = (rates * tangent_pred, counts[part, :].astype(F32) - rates)
-        total = jnp.zeros((CHUNK, 2 * rows), F32)
-        for n in range(2 * covs):
-            head, rest = split(covar[n % covs, part, :] * factors[n // covs])
-            value = bf16_dot(jnp.concatenate([head, rest], axis=0), time_cols[...])
-            total = jnp.where(which == n, value[:CHUNK] + value[CHUNK:], total)
-        total = total + pltpu.roll(total, rows, 1)
-        head, rest = split_wide(total)
-        back[:, part] = jnp.where(lane < rows, head, rest).T.astype(BF16)
+            head, rest = split(covar[n % covs, :, part] * factors[n // covs])
+            value = bf16_dot(jnp.concatenate([head, rest], axis=0), time_cols[part])
+            sums = jnp.where(which == n, value[:cd] + value[cd:], sums)
+        total = total + sums
+    total = total + pltpu.roll(total, rows, 1)
+    head, rest = split_wide(total)
+    back[...] = jnp.where(lane < rows, head, rest).T.astype(BF16)
 
     def backward(i, dt, dc):
         src_t = {0: pl.ds(0, td), 1: pl.ds(td + HT, HT), -1: pl.ds(td, HT)}[dt]

time: 17.5 us -> 17.5 us (level)
  no operation moved by 1% of the time
where the time goes in v6:
time: 17.5 us; the launch traced here: 17.2 us
  Pallas kernels  15.3 us (87%)
  local copies, waits for them, and re-layouts  1.33 us (8%)
  between operations  0.64 us (4%)
    pallas_call x1, Pallas kernels, body(): pl.pallas_call(functools.partial(kernel, nt, nc), out_shape=jax.ShapeDtyp...  15.3 us
    squeeze x1, local copies, waits for them, and re-layouts, body(): return (out[0], out[1])  1.33 us

profile of v6, /device:TPU:1, one launch (start us, length us, event | category | flops | bytes accessed | tf_op | source)
XLA Modules:
  0.0 17.2 jit_solution(8480194565558812482)
XLA Ops:
  0.6 15.3 %hessian_product.1 = f32[2,3,4,256]{3,2,1,0:T(4,128)} custom-call(f32[3,4,256]{2,1,0:T(4,128)} %bitcast.10, f32[3,4,256]{2,1,0:T(4,128)} %bitcast.11, f32[3,512,512]{2,1,0:T(8,128)} %covar_h.1, s32[512,512]{1,0:T(8,128)} %counts_h.1, s32[1,512]{1,0:T(1,128)} %bitcast.12, f32[16,512]{1,0:T(8,128)} %sweight_h.1, s32[1,512]{1,0:T(1,128)} %bitcast.13, ...), custom_call_target="tpu_custom_call" | custom-call | tf_op jit(solution)/shard_map/hessian_product/pallas_call | solution.py:261
  15.9 1.3 %slice_bitcast_fusion = (f32[3,256,4]{1,2,0:T(4,128)}, f32[3,256,4]{1,2,0:T(4,128)}) fusion(f32[2,3,256,4]{2,3,1,0:T(4,128)} %bitcast.9), kind=kLoop, calls=%fused_computation | loop fusion | bytes 49152 | tf_op jit(solution)/shard_map/squeeze | solution.py:290

commit v7 on v6

--- a/solution.py
+++ b/solution.py
@@ -13,7 +13,7 @@
 SUB = 8
 CHUNK = 256
 MESH = pl.DeviceIdType.MESH
-DIRS = [(dt, dc) for dt in (1, -1, 0) for dc in (0, 1, -1) if (dt, dc) != (0, 0)]
+DIRS = [(1, 1), (1, -1), (-1, 1), (-1, -1), (0, 1), (0, -1), (1, 0), (-1, 0)]
 F32 = jnp.float32
 BF16 = jnp.bfloat16
 
@@ -33,7 +33,7 @@
 
 
 def kernel(
-    nt, nc, theta_h, tangent_h, covar_h, counts_h, sfirst_h, sweight_h, tfirst_h, tweight_h, out_ref,
+    nt, nc, theta_h, tangent_h, covar_h, counts_h, sfirst_h, sweight_h, tfirst_h, tweight_h, hess_ref, grad_ref,
     theta, tangent, covar, counts, sfirst, sweight, tfirst, tweight,
     own, low, high, space, time_rows, time_cols, back,
     res_own, res_edge, got, load_sem, send_sem, recv_sem, back_send, back_recv,
@@ -237,7 +237,7 @@
     for p in range(2):
         scale = F32((sweight.shape[0] if p == 0 else 1) * (hd // td))
         for k in range(covs):
-            out_ref[p, k] = total[:, p * covs + k, :] / scale
+            (grad_ref if p else hess_ref)[k] = total[:, p * covs + k, :] / scale
 
     for i, (dt, dc) in enumerate(DIRS):
         @pl.when(there(dt, dc))
@@ -260,9 +260,9 @@
     dirs = len(DIRS)
     out = pl.pallas_call(
         functools.partial(kernel, nt, nc),
-        out_shape=jax.ShapeDtypeStruct((2, covs, td, sd), F32),
+        out_shape=[jax.ShapeDtypeStruct((covs, td, sd), F32)] * 2,
         in_specs=[pl.BlockSpec(memory_space=pltpu.HBM)] * len(operands),
-        out_specs=pl.BlockSpec(memory_space=pltpu.VMEM),
+        out_specs=[pl.BlockSpec(memory_space=pltpu.VMEM)] * 2,
         scratch_shapes=[pltpu.VMEM(x.shape, x.dtype) for x in operands]
         + [
             pltpu.VMEM((te, SUB, sd), F32),
@@ -286,8 +286,7 @@
         ),
         name="hessian_product",
     )(*operands)
-    out = out.transpose(0, 1, 3, 2)
-    return out[0], out[1]
+    return tuple(value.transpose(0, 2, 1) for value in out)
 
 
 def solution(mesh):

time: 17.5 us -> 18.9 us (1.080)
  local copies, waits for them, and re-layouts: 1.33 us -> 2.61 us
    unnamed x0 -> x2, local copies, waits for them, and re-layouts: none -> 2.61 us
    squeeze x1 -> x0, local copies, waits for them, and re-layouts: 1.33 us -> none  [body(): return (out[0], out[1])]
where the time goes in v7:
time: 18.9 us; the launch traced here: 18.5 us
  Pallas kernels  15.3 us (81%)
  local copies, waits for them, and re-layouts  2.61 us (14%)
  between operations  0.64 us (3%)
    pallas_call x1, Pallas kernels, body(): pl.pallas_call(functools.partial(kernel, nt, nc), out_shape=[jax.ShapeDty...  15.3 us
    unnamed x2, local copies, waits for them, and re-layouts  2.61 us

profile of v7, /device:TPU:1, one launch (start us, length us, event | category | flops | bytes accessed | tf_op | source)
XLA Modules:
  0.0 18.5 jit_solution(5131040854097457472)
XLA Ops:
  0.6 15.3 %hessian_product.1 = (f32[3,4,256]{2,1,0:T(4,128)}, f32[3,4,256]{2,1,0:T(4,128)}) custom-call(f32[3,4,256]{2,1,0:T(4,128)} %bitcast.6, f32[3,4,256]{2,1,0:T(4,128)} %bitcast.7, f32[3,512,512]{2,1,0:T(8,128)} %covar_h.1, s32[512,512]{1,0:T(8,128)} %counts_h.1, s32[1,512]{1,0:T(1,128)} %bitcast.10, f32[16,512]{1,0:T(8,128)} %sweight_h.1, s32[1,512]{1,0:T(1,128)} %bitcast.11, ...), custom_call_target="tpu_custom_call" | custom-call | tf_op jit(solution)/shard_map/hessian_product/pallas_call | solution.py:261
  15.9 1.3 %copy.12 = f32[3,256,4]{1,2,0:T(4,128)} copy(f32[3,256,4]{1,2,0:T(4,128)} %bitcast.9) | data formatting | bytes 24576
  17.2 1.3 %copy.13 = f32[3,256,4]{1,2,0:T(4,128)} copy(f32[3,256,4]{1,2,0:T(4,128)} %bitcast.8) | data formatting | bytes 24576

commit v8 on v6

--- a/solution.py
+++ b/solution.py
@@ -13,7 +13,7 @@
 SUB = 8
 CHUNK = 256
 MESH = pl.DeviceIdType.MESH
-DIRS = [(dt, dc) for dt in (1, -1, 0) for dc in (0, 1, -1) if (dt, dc) != (0, 0)]
+DIRS = [(1, 1), (1, -1), (-1, 1), (-1, -1), (0, 1), (0, -1), (1, 0), (-1, 0)]
 F32 = jnp.float32
 BF16 = jnp.bfloat16
 
@@ -78,9 +78,6 @@
         pltpu.make_async_copy(covar_h, covar, load_sem.at[6]),
         pltpu.make_async_copy(counts_h, counts, load_sem.at[7]),
     ]
-    for copy in chunk_loads:
-        copy.start()
-
     loads[0].wait()
     loads[1].wait()
     for p, ref in enumerate((theta, tangent)):
@@ -105,6 +102,9 @@
         @pl.when(there(dt, dc))
         def _(i=i, dt=dt, dc=dc):
             forward(i, dt, dc).start()
+
+    for copy in chunk_loads:
+        copy.start()
 
     loads[2].wait()
     loads[3].wait()

time: 17.5 us -> 17.5 us (level)
  no operation moved by 1% of the time
where the time goes in v8:
time: 17.5 us; the launch traced here: 17.2 us
  Pallas kernels  15.3 us (87%)
  local copies, waits for them, and re-layouts  1.33 us (8%)
  between operations  0.64 us (4%)
    pallas_call x1, Pallas kernels, body(): pl.pallas_call(functools.partial(kernel, nt, nc), out_shape=jax.ShapeDtyp...  15.3 us
    squeeze x1, local copies, waits for them, and re-layouts, body(): return (out[0], out[1])  1.33 us

profile of v8, /device:TPU:1, one launch (start us, length us, event | category | flops | bytes accessed | tf_op | source)
XLA Modules:
  0.0 17.2 jit_solution(10324295542940503080)
XLA Ops:
  0.6 15.3 %hessian_product.1 = f32[2,3,4,256]{3,2,1,0:T(4,128)} custom-call(f32[3,4,256]{2,1,0:T(4,128)} %bitcast.10, f32[3,4,256]{2,1,0:T(4,128)} %bitcast.11, f32[3,512,512]{2,1,0:T(8,128)} %covar_h.1, s32[512,512]{1,0:T(8,128)} %counts_h.1, s32[1,512]{1,0:T(1,128)} %bitcast.12, f32[16,512]{1,0:T(8,128)} %sweight_h.1, s32[1,512]{1,0:T(1,128)} %bitcast.13, ...), custom_call_target="tpu_custom_call" | custom-call | tf_op jit(solution)/shard_map/hessian_product/pallas_call | solution.py:261
  15.9 1.3 %slice_bitcast_fusion = (f32[3,256,4]{1,2,0:T(4,128)}, f32[3,256,4]{1,2,0:T(4,128)}) fusion(f32[2,3,256,4]{2,3,1,0:T(4,128)} %bitcast.9), kind=kLoop, calls=%fused_computation | loop fusion | bytes 49152 | tf_op jit(solution)/shard_map/squeeze | solution.py:290
